TPU v7x, 512 devices: a whole 4x4x16 slice. The times are simulated.
512 devices in a mesh: grp: 16 (over y, x), tile: 32 (over z, core).
Axes of the slice: x: 4, y: 4, z: 16, core: 2. Of those that a mesh axis runs over, the one named last changes fastest.
Arguments:
- latent: bfloat16 [8, 64, 64, 512], P(None, 'grp', 'tile'), may hold values from -36 to 36
- coarse_filters: bfloat16 [3, 3, 3, 512, 512], P(None, None, None, None, 'grp'), may hold values from -0.0546875 to 0.0546875
- mid_filters: bfloat16 [3, 3, 3, 256, 256], P(None, None, None, None, 'tile'), may hold values from -0.078125 to 0.078125
- fine_filters: bfloat16 [3, 3, 3, 128, 128], replicated, may hold values from -0.109375 to 0.109375
- coarse_proj: bfloat16 [512, 256], replicated, may hold values from -0.25 to 0.25
- mid_proj: bfloat16 [256, 128], replicated, may hold values from -0.375 to 0.375
Outputs:
- frames_out: bfloat16 [8, 256, 256, 128], P(None, 'grp', 'tile')
All inputs are finite; a program needn't handle non-finite values.
Results may differ from a plain program's by a relative error of at most 0.018.
Values may be sent and summed in bfloat16 or wider, within the bound.
A program may use at most 128 MiB of HBM per device.

v0:
```python
import jax
import jax.numpy as jnp
from jax import lax
from jax.sharding import PartitionSpec as P


def with_halo(shard, sides, width):
    for axis, dim in sides:
        size, length = (lax.axis_size(axis), shard.shape[dim])
        up = [(i, (i + 1) % size) for i in range(size - 1)]
        down = [(j, i) for i, j in up]
        last = lax.slice_in_dim(shard, length - width, length, axis=dim)
        initial = lax.slice_in_dim(shard, 0, width, axis=dim)
        before = lax.ppermute(last, axis, up)
        after = lax.ppermute(initial, axis, down)
        shard = jnp.concatenate([before, shard, after], axis=dim)
    return shard


def activate(values):
    widened = values.astype(jnp.float32)
    scaled = widened * lax.rsqrt(jnp.mean(widened * widened, axis=-1, keepdims=True) + 1e-06)
    return jax.nn.silu(scaled).astype(jnp.bfloat16)


def double_size(values):
    return jnp.repeat(jnp.repeat(values, 2, axis=1), 2, axis=2)


def time_padded(values):
    return jnp.pad(values, ((2, 0), (0, 0), (0, 0), (0, 0)))


def stencil_columns(extended):
    padded = time_padded(extended)
    height = extended.shape[1] - 2
    breadth = extended.shape[2] - 2
    return jnp.concatenate(
        [
            padded[:, row_step : row_step + height, col_step : col_step + breadth, :]
            for row_step in range(3)
            for col_step in range(3)
        ],
        axis=-1,
    )


def apply_columns(columns, filters):
    frames = columns.shape[0] - 2
    folded = filters.reshape(3, 9 * filters.shape[3], filters.shape[4])
    total = jnp.dot(columns[0:frames], folded[0], preferred_element_type=jnp.float32)
    for frame_step in (1, 2):
        total = total + jnp.dot(
            columns[frame_step : frame_step + frames],
            folded[frame_step],
            preferred_element_type=jnp.float32,
        )
    return total


def coarse_conv(extended, filters):
    padded = time_padded(extended)
    frames = extended.shape[0]
    height = extended.shape[1] - 2
    breadth = extended.shape[2] - 2
    inputs = filters.shape[3]
    outputs = filters.shape[4]
    total = jnp.zeros((frames, height, breadth, outputs), jnp.float32)
    for frame_step in range(3):
        spread = jnp.transpose(filters[frame_step], (2, 0, 1, 3)).reshape(inputs, 9 * outputs)
        products = jnp.dot(
            padded[frame_step : frame_step + frames], spread, preferred_element_type=jnp.float32
        )
        for row_step in range(3):
            for col_step in range(3):
                lane = 3 * row_step + col_step
                total = (
                    total
                    + products[
                        :,
                        row_step : row_step + height,
                        col_step : col_step + breadth,
                        lane * outputs : (lane + 1) * outputs,
                    ]
                )
    return total


def middle_conv(extended, mid_filters):
    columns = stencil_columns(extended)
    return apply_columns(columns, lax.all_gather(mid_filters, "tile", axis=4, tiled=True))


def body(latent, coarse_filters, mid_filters, fine_filters, coarse_proj, mid_proj):
    first_act = activate(latent)
    whole = lax.all_gather(first_act, "grp", axis=1, tiled=True)
    widened = with_halo(whole, (("tile", 2),), 1)
    padded = jnp.pad(widened, ((0, 0), (1, 1), (0, 0), (0, 0)))
    filtered = coarse_conv(padded, coarse_filters).astype(jnp.bfloat16)
    returned = lax.all_to_all(filtered, "grp", split_axis=1, concat_axis=3, tiled=True)
    level_zero = (latent.astype(jnp.float32) + returned.astype(jnp.float32)).astype(jnp.bfloat16)
    reduced = jnp.dot(level_zero, coarse_proj, preferred_element_type=jnp.float32).astype(
        jnp.bfloat16
    )
    mid_act = double_size(activate(reduced))
    mid_ext = with_halo(mid_act, (("grp", 1), ("tile", 2)), 1)
    mid_terms = middle_conv(mid_ext, mid_filters)
    mid_out = (double_size(reduced).astype(jnp.float32) + mid_terms).astype(jnp.bfloat16)
    fine_low = jnp.dot(mid_out, mid_proj, preferred_element_type=jnp.float32).astype(jnp.bfloat16)
    fine_in = double_size(fine_low)
    fine_act = double_size(activate(fine_low))
    fine_ext = with_halo(fine_act, (("grp", 1), ("tile", 2)), 1)
    fine_terms = apply_columns(stencil_columns(fine_ext), fine_filters)
    return (fine_in.astype(jnp.float32) + fine_terms).astype(jnp.bfloat16)


def solution(mesh):
    in_specs = (
        P(None, "grp", "tile", None),
        P(None, None, None, None, "grp"),
        P(None, None, None, None, "tile"),
        P(),
        P(),
        P(),
    )
    out_specs = P(None, "grp", "tile", None)
    return jax.shard_map(body, mesh=mesh, in_specs=in_specs, out_specs=out_specs, check_vma=False)
```

profile of v0, /device:TPU:7, one launch (start us, length us, event | category | flops | bytes accessed | tf_op | source)
XLA Modules:
  0.0 200.4 jit_solution(11646952750403236550)
XLA Ops:
  7.6 1.6 fusion.33
  10.0 61.1 %all-gather.3.cloned.1.call-done = bf16[8,64,2,512]{3,0,2,1:T(8,128)(2,1)} async-done(((bf16[8,4,2,512]{3,0,2,1:T(8,128)(2,1)}), bf16[8,64,2,512]{3,0,2,1:T(8,128)(2,1)}) %all-gather.3.cloned.1.call-update) | async-done | bytes 1048592 | tf_op jit(solution)/shard_map/all_gather | solution.py:96
  71.1 1.8 copy.25
  73.0 5.1 %collective-permute-start = (bf16[8,64,1,512]{3,1,2,0:T(8,128)(2,1)S(1)}, bf16[8,64,1,512]{3,1,2,0:T(8,128)(2,1)S(1)}, u32[]{:S(2)}, u32[]{:S(2)}) collective-permute-start(bf16[8,64,1,512]{3,1,2,0:T(8,128)(2,1)S(1)} %get-tuple-element.8), channel_id=1, source_target_pairs={{0,1},{1,2},{2,3},{3,4},{4,5},{5,6},{6,7},{7,8},{8,9},{9,10},{10,1... | collective-permute-start | bytes 1572872 | tf_op jit(solution)/shard_map/ppermute | solution.py:14
  78.0 1.9 collective-permute-start.1
  80.0 4.1 %collective-permute-done = bf16[8,64,1,512]{3,1,2,0:T(8,128)(2,1)S(1)} collective-permute-done((bf16[8,64,1,512]{3,1,2,0:T(8,128)(2,1)S(1)}, bf16[8,64,1,512]{3,1,2,0:T(8,128)(2,1)S(1)}, u32[]{:S(2)}, u32[]{:S(2)}) %collective-permute-start) | collective-permute-done | bytes 524320 | tf_op jit(solution)/shard_map/ppermute | solution.py:14
  84.1 4.4 %collective-permute-done.1 = bf16[8,64,1,512]{3,1,2,0:T(8,128)(2,1)S(1)} collective-permute-done((bf16[8,64,1,512]{3,1,2,0:T(8,128)(2,1)S(1)}, bf16[8,64,1,512]{3,1,2,0:T(8,128)(2,1)S(1)}, u32[]{:S(2)}, u32[]{:S(2)}) %collective-permute-start.1) | collective-permute-done | bytes 524320 | tf_op jit(solution)/shard_map/ppermute | solution.py:15
  89.6 1.4 fusion.47
  91.0 1.4 fusion.50
  92.5 1.4 fusion.51
  93.9 2.5 %fusion.24 = bf16[8,64,2,32]{3,1,2,0:T(8,128)(2,1)S(1)} fusion(f32[8,66,4,288]{3,1,2,0:T(8,128)S(1)} %fusion.47, f32[8,66,4,288]{3,1,2,0:T(8,128)S(1)} %fusion.51, f32[8,66,4,288]{3,1,2,0:T(8,128)S(1)} %fusion.50), kind=kLoop, calls=%fused_computation.35 | loop fusion | flops 884736 | bytes 3604480 | tf_op jit(solution)/shard_map/convert_element_type | solution.py:99
  97.0 9.8 %all_to_all.4 = bf16[16,2,1024]{2,1,0:T(2,128)(2,1)S(1)} all-to-all(bf16[16,2,1024]{2,1,0:T(2,128)(2,1)S(1)} %reshape.91), channel_id=1, replica_groups=mesh['grp'=16,'tile'=32] {'grp'}, dimensions={0} | all-to-all | bytes 131072 | tf_op jit(solution)/shard_map/all_to_all | solution.py:100
  108.0 3.7 %collective-permute-start.2 = (bf16[8,1,4,256]{3,2,1,0:T(4,128)(2,1)S(1)}, bf16[8,1,4,256]{3,2,1,0:T(4,128)(2,1)S(1)}, u32[]{:S(2)}, u32[]{:S(2)}) collective-permute-start(bf16[8,1,4,256]{3,2,1,0:T(4,128)(2,1)S(1)} %get-tuple-element.23), channel_id=1, source_target_pairs={{0,32},{32,64},{64,96},{96,128},{128,160},{160,192},{192,224},{224... | collective-permute-start | bytes 49160 | tf_op jit(solution)/shard_map/ppermute | solution.py:14
  111.7 1.9 collective-permute-start.3
  113.7 4.6 %collective-permute-done.3 = bf16[8,1,4,256]{3,2,1,0:T(4,128)(2,1)S(1)} collective-permute-done((bf16[8,1,4,256]{3,2,1,0:T(4,128)(2,1)S(1)}, bf16[8,1,4,256]{3,2,1,0:T(4,128)(2,1)S(1)}, u32[]{:S(2)}, u32[]{:S(2)}) %collective-permute-start.3) | collective-permute-done | bytes 16416 | tf_op jit(solution)/shard_map/ppermute | solution.py:15
  118.4 4.6 %collective-permute-start.4 = (bf16[8,10,1,256]{3,2,1,0:T(2,128)(2,1)S(1)}, bf16[8,10,1,256]{3,2,1,0:T(2,128)(2,1)S(1)}, u32[]{:S(2)}, u32[]{:S(2)}) collective-permute-start(bf16[8,10,1,256]{3,2,1,0:T(2,128)(2,1)S(1)} %get-tuple-element.20), channel_id=1, source_target_pairs={{0,1},{1,2},{2,3},{3,4},{4,5},{5,6},{6,7},{7,8},{8,9},{9,10},{10,1... | collective-permute-start | bytes 122888 | tf_op jit(solution)/shard_map/ppermute | solution.py:14
  123.1 2.1 %collective-permute-start.5 = (bf16[8,10,1,256]{3,2,1,0:T(2,128)(2,1)S(1)}, bf16[8,10,1,256]{3,2,1,0:T(2,128)(2,1)S(1)}, u32[]{:S(2)}, u32[]{:S(2)}) collective-permute-start(bf16[8,10,1,256]{3,2,1,0:T(2,128)(2,1)S(1)} %get-tuple-element.21), channel_id=1, source_target_pairs={{1,0},{2,1},{3,2},{4,3},{5,4},{6,5},{7,6},{8,7},{9,8},{10,9},{11,1... | collective-permute-start | bytes 122888 | tf_op jit(solution)/shard_map/ppermute | solution.py:15
  125.6 3.7 %collective-permute-done.5 = bf16[8,10,1,256]{3,2,1,0:T(2,128)(2,1)S(1)} collective-permute-done((bf16[8,10,1,256]{3,2,1,0:T(2,128)(2,1)S(1)}, bf16[8,10,1,256]{3,2,1,0:T(2,128)(2,1)S(1)}, u32[]{:S(2)}, u32[]{:S(2)}) %collective-permute-start.5) | collective-permute-done | bytes 40992 | tf_op jit(solution)/shard_map/ppermute | solution.py:15
  136.8 16.2 %all-gather.5.cloned.1.call-done = bf16[3,3,3,256,256]{3,4,2,1,0:T(8,128)(2,1)} async-done(((bf16[3,3,3,256,8]{3,4,2,1,0:T(8,128)(2,1)}), bf16[3,3,3,256,256]{3,4,2,1,0:T(8,128)(2,1)}) %all-gather.5.cloned.1.call-update) | async-done | bytes 3538960 | tf_op jit(solution)/shard_map/all_gather | solution.py:91
  153.0 3.3 %fusion.40 = (bf16[1,3,3,256,256]{3,4,2,1,0:T(8,128)(2,1)S(1)}, bf16[1,3,3,256,256]{3,4,2,1,0:T(8,128)(2,1)S(1)}, bf16[1,3,3,256,256]{3,4,2,1,0:T(8,128)(2,1)}) fusion(bf16[3,3,3,256,256]{3,4,2,1,0:T(8,128)(2,1)} %all-gather.5.cloned.1.call-done), kind=kLoop, calls=%fused_computation.110 | loop fusion | bytes 7077888 | tf_op jit(solution)/shard_map/slice | solution.py:55
  156.3 2.4 %copy.49 = bf16[1,3,3,256,256]{4,3,2,1,0:T(8,128)(2,1)} copy(bf16[1,3,3,256,256]{3,4,2,1,0:T(8,128)(2,1)} %get-tuple-element.7) | data formatting | bytes 2359296
  158.7 1.6 copy.50
  161.0 2.4 %fusion.48 = f32[8,8,4,256]{3,2,1,0:T(4,128)S(1)} fusion(bf16[10,8,4,2304]{3,2,1,0:T(4,128)(2,1)} %slice_dynamic-update-slice_fusion.9, bf16[2304,256,1,1]{1,0,3,2:T(8,128)(2,1)} %bitcast.115), kind=kOutput, calls=%fused_computation.119 | convolution fusion | flops 301989888 | bytes 2916352 | tf_op jit(solution)/shard_map/dot_general | solution.py:51
  163.4 2.0 convolution_add_fusion.3
  165.4 2.1 %fusion.14 = bf16[8,8,4,256]{3,2,1,0:T(4,128)(2,1)S(1)} fusion(f32[8,8,4,256]{3,2,1,0:T(4,128)S(1)} %convert_element_type.86, f32[8,8,4,256]{3,2,1,0:T(4,128)S(1)} %convolution_add_fusion.3, bf16[10,8,4,2304]{3,2,1,0:T(4,128)(2,1)} %slice_dynamic-update-slice_fusion.9, bf16[2304,256,1,1]{1,0,3,2:T(8,128)(2,1)S(1)} %bitcast.114), kind=kOutput, calls=%fused_computation.21 | convolution fusion | flops 302186496 | bytes 3309568 | tf_op jit(solution)/shard_map/dot_general | solution.py:53
  168.2 2.7 %collective-permute-start.6 = (bf16[8,1,8,128]{3,2,1,0:T(8,128)(2,1)S(1)}, bf16[8,1,8,128]{3,2,1,0:T(8,128)(2,1)S(1)}, u32[]{:S(2)}, u32[]{:S(2)}) collective-permute-start(bf16[8,1,8,128]{3,2,1,0:T(8,128)(2,1)S(1)} %get-tuple-element.18), channel_id=1, source_target_pairs={{0,32},{32,64},{64,96},{96,128},{128,160},{160,192},{192,224},{224... | collective-permute-start | bytes 49160 | tf_op jit(solution)/shard_map/ppermute | solution.py:14
  170.9 2.6 %collective-permute-start.7 = (bf16[8,1,8,128]{3,2,1,0:T(8,128)(2,1)S(1)}, bf16[8,1,8,128]{3,2,1,0:T(8,128)(2,1)S(1)}, u32[]{:S(2)}, u32[]{:S(2)}) collective-permute-start(bf16[8,1,8,128]{3,2,1,0:T(8,128)(2,1)S(1)} %get-tuple-element.19), channel_id=1, source_target_pairs={{32,0},{64,32},{96,64},{128,96},{160,128},{192,160},{224,192},{256... | collective-permute-start | bytes 49160 | tf_op jit(solution)/shard_map/ppermute | solution.py:15
  173.5 4.0 %collective-permute-done.7 = bf16[8,1,8,128]{3,2,1,0:T(8,128)(2,1)S(1)} collective-permute-done((bf16[8,1,8,128]{3,2,1,0:T(8,128)(2,1)S(1)}, bf16[8,1,8,128]{3,2,1,0:T(8,128)(2,1)S(1)}, u32[]{:S(2)}, u32[]{:S(2)}) %collective-permute-start.7) | collective-permute-done | bytes 16416 | tf_op jit(solution)/shard_map/ppermute | solution.py:15
  177.6 5.2 %collective-permute-start.8 = (bf16[8,18,1,128]{3,2,1,0:T(2,128)(2,1)S(1)}, bf16[8,18,1,128]{3,2,1,0:T(2,128)(2,1)S(1)}, u32[]{:S(2)}, u32[]{:S(2)}) collective-permute-start(bf16[8,18,1,128]{3,2,1,0:T(2,128)(2,1)S(1)} %get-tuple-element.16), channel_id=1, source_target_pairs={{0,1},{1,2},{2,3},{3,4},{4,5},{5,6},{6,7},{7,8},{8,9},{9,10},{10,1... | collective-permute-start | bytes 110600 | tf_op jit(solution)/shard_map/ppermute | solution.py:14
  182.9 1.9 collective-permute-start.9
  184.9 3.6 %collective-permute-done.9 = bf16[8,18,1,128]{3,2,1,0:T(2,128)(2,1)S(1)} collective-permute-done((bf16[8,18,1,128]{3,2,1,0:T(2,128)(2,1)S(1)}, bf16[8,18,1,128]{3,2,1,0:T(2,128)(2,1)S(1)}, u32[]{:S(2)}, u32[]{:S(2)}) %collective-permute-start.9) | collective-permute-done | bytes 36896 | tf_op jit(solution)/shard_map/ppermute | solution.py:15
  192.0 1.5 fusion.12
  (81 shorter events, 17.8 us)
Async XLA Ops:
  6.5 100.8 %copy-start = (bf16[512,256]{1,0:T(8,128)(2,1)S(1)}, bf16[512,256]{1,0:T(8,128)(2,1)}, u32[]{:S(2)}) copy-start(bf16[512,256]{1,0:T(8,128)(2,1)} %param.10) | copy-start | bytes 786436
  6.5 73.4 %copy-start.2 = (bf16[3,3,3,512,32]{3,4,2,1,0:T(8,128)(2,1)S(1)}, bf16[3,3,3,512,32]{3,4,2,1,0:T(8,128)(2,1)}, u32[]{:S(2)}) copy-start(bf16[3,3,3,512,32]{3,4,2,1,0:T(8,128)(2,1)} %param.7) | copy-start | bytes 2654212
  6.5 64.5 %all-gather.3.cloned.1.call-start = ((), (), s32[]{:S(2)}) async-start(), calls=%async_computation.1 | async-start | bytes 1114112 | tf_op jit(solution)/shard_map/all_gather | solution.py:96
  9.2 143.8 %all-gather.5.cloned.1.call-start = ((), (), s32[]{:S(2)}) async-start(), calls=%async_computation.2 | async-start | bytes 3649536 | tf_op jit(solution)/shard_map/all_gather | solution.py:91
  73.0 11.2 %collective-permute-start = (bf16[8,64,1,512]{3,1,2,0:T(8,128)(2,1)S(1)}, bf16[8,64,1,512]{3,1,2,0:T(8,128)(2,1)S(1)}, u32[]{:S(2)}, u32[]{:S(2)}) collective-permute-start(bf16[8,64,1,512]{3,1,2,0:T(8,128)(2,1)S(1)} %get-tuple-element.8), channel_id=1, source_target_pairs={{0,1},{1,2},{2,3},{3,4},{4,5},{5,6},{6,7},{7,8},{8,9},{9,10},{10,1... | collective-permute-start | bytes 1572872 | tf_op jit(solution)/shard_map/ppermute | solution.py:14
  78.0 10.5 %collective-permute-start.1 = (bf16[8,64,1,512]{3,1,2,0:T(8,128)(2,1)S(1)}, bf16[8,64,1,512]{3,1,2,0:T(8,128)(2,1)S(1)}, u32[]{:S(2)}, u32[]{:S(2)}) collective-permute-start(bf16[8,64,1,512]{3,1,2,0:T(8,128)(2,1)S(1)} %get-tuple-element.9), channel_id=1, source_target_pairs={{1,0},{2,1},{3,2},{4,3},{5,4},{6,5},{7,6},{8,7},{9,8},{10,9},{11,1... | collective-permute-start | bytes 1572872 | tf_op jit(solution)/shard_map/ppermute | solution.py:15
  96.4 10.9 %copy-start.4 = (bf16[8,4,2,512]{3,2,1,0:T(2,128)(2,1)S(1)}, bf16[8,4,2,512]{3,2,1,0:T(2,128)(2,1)}, u32[]{:S(2)}) copy-start(bf16[8,4,2,512]{3,2,1,0:T(2,128)(2,1)} %param.6) | copy-start | bytes 196612
  108.0 5.6 %collective-permute-start.2 = (bf16[8,1,4,256]{3,2,1,0:T(4,128)(2,1)S(1)}, bf16[8,1,4,256]{3,2,1,0:T(4,128)(2,1)S(1)}, u32[]{:S(2)}, u32[]{:S(2)}) collective-permute-start(bf16[8,1,4,256]{3,2,1,0:T(4,128)(2,1)S(1)} %get-tuple-element.23), channel_id=1, source_target_pairs={{0,32},{32,64},{64,96},{96,128},{128,160},{160,192},{192,224},{224... | collective-permute-start | bytes 49160 | tf_op jit(solution)/shard_map/ppermute | solution.py:14
  111.7 6.6 %collective-permute-start.3 = (bf16[8,1,4,256]{3,2,1,0:T(4,128)(2,1)S(1)}, bf16[8,1,4,256]{3,2,1,0:T(4,128)(2,1)S(1)}, u32[]{:S(2)}, u32[]{:S(2)}) collective-permute-start(bf16[8,1,4,256]{3,2,1,0:T(4,128)(2,1)S(1)} %get-tuple-element.22), channel_id=1, source_target_pairs={{32,0},{64,32},{96,64},{128,96},{160,128},{192,160},{224,192},{256... | collective-permute-start | bytes 49160 | tf_op jit(solution)/shard_map/ppermute | solution.py:15
  118.4 7.2 %collective-permute-start.4 = (bf16[8,10,1,256]{3,2,1,0:T(2,128)(2,1)S(1)}, bf16[8,10,1,256]{3,2,1,0:T(2,128)(2,1)S(1)}, u32[]{:S(2)}, u32[]{:S(2)}) collective-permute-start(bf16[8,10,1,256]{3,2,1,0:T(2,128)(2,1)S(1)} %get-tuple-element.20), channel_id=1, source_target_pairs={{0,1},{1,2},{2,3},{3,4},{4,5},{5,6},{6,7},{7,8},{8,9},{9,10},{10,1... | collective-permute-start | bytes 122888 | tf_op jit(solution)/shard_map/ppermute | solution.py:14
  123.1 6.3 %collective-permute-start.5 = (bf16[8,10,1,256]{3,2,1,0:T(2,128)(2,1)S(1)}, bf16[8,10,1,256]{3,2,1,0:T(2,128)(2,1)S(1)}, u32[]{:S(2)}, u32[]{:S(2)}) collective-permute-start(bf16[8,10,1,256]{3,2,1,0:T(2,128)(2,1)S(1)} %get-tuple-element.21), channel_id=1, source_target_pairs={{1,0},{2,1},{3,2},{4,3},{5,4},{6,5},{7,6},{8,7},{9,8},{10,9},{11,1... | collective-permute-start | bytes 122888 | tf_op jit(solution)/shard_map/ppermute | solution.py:15
  161.0 2.4 %copy-start.1 = (bf16[1,3,3,256,256]{4,3,2,1,0:T(8,128)(2,1)S(1)}, bf16[1,3,3,256,256]{4,3,2,1,0:T(8,128)(2,1)}, u32[]{:S(2)}) copy-start(bf16[1,3,3,256,256]{4,3,2,1,0:T(8,128)(2,1)} %copy.50) | copy-start | bytes 3538948
  165.4 2.1 %copy-start.5 = (bf16[256,128]{1,0:T(8,128)(2,1)S(1)}, bf16[256,128]{1,0:T(8,128)(2,1)}, u32[]{:S(2)}) copy-start(bf16[256,128]{1,0:T(8,128)(2,1)} %param.11) | copy-start | bytes 196612
  165.4 19.4 %copy-start.3 = (bf16[3,3,3,128,128]{4,3,2,1,0:T(8,128)(2,1)S(1)}, bf16[3,3,3,128,128]{4,3,2,1,0:T(8,128)(2,1)}, u32[]{:S(2)}) copy-start(bf16[3,3,3,128,128]{4,3,2,1,0:T(8,128)(2,1)} %param.9) | copy-start | bytes 2654212
  168.2 5.3 %collective-permute-start.6 = (bf16[8,1,8,128]{3,2,1,0:T(8,128)(2,1)S(1)}, bf16[8,1,8,128]{3,2,1,0:T(8,128)(2,1)S(1)}, u32[]{:S(2)}, u32[]{:S(2)}) collective-permute-start(bf16[8,1,8,128]{3,2,1,0:T(8,128)(2,1)S(1)} %get-tuple-element.18), channel_id=1, source_target_pairs={{0,32},{32,64},{64,96},{96,128},{128,160},{160,192},{192,224},{224... | collective-permute-start | bytes 49160 | tf_op jit(solution)/shard_map/ppermute | solution.py:14
  170.9 6.6 %collective-permute-start.7 = (bf16[8,1,8,128]{3,2,1,0:T(8,128)(2,1)S(1)}, bf16[8,1,8,128]{3,2,1,0:T(8,128)(2,1)S(1)}, u32[]{:S(2)}, u32[]{:S(2)}) collective-permute-start(bf16[8,1,8,128]{3,2,1,0:T(8,128)(2,1)S(1)} %get-tuple-element.19), channel_id=1, source_target_pairs={{32,0},{64,32},{96,64},{128,96},{160,128},{192,160},{224,192},{256... | collective-permute-start | bytes 49160 | tf_op jit(solution)/shard_map/ppermute | solution.py:15
  177.6 7.3 %collective-permute-start.8 = (bf16[8,18,1,128]{3,2,1,0:T(2,128)(2,1)S(1)}, bf16[8,18,1,128]{3,2,1,0:T(2,128)(2,1)S(1)}, u32[]{:S(2)}, u32[]{:S(2)}) collective-permute-start(bf16[8,18,1,128]{3,2,1,0:T(2,128)(2,1)S(1)} %get-tuple-element.16), channel_id=1, source_target_pairs={{0,1},{1,2},{2,3},{3,4},{4,5},{5,6},{6,7},{7,8},{8,9},{9,10},{10,1... | collective-permute-start | bytes 110600 | tf_op jit(solution)/shard_map/ppermute | solution.py:14
  182.9 5.7 %collective-permute-start.9 = (bf16[8,18,1,128]{3,2,1,0:T(2,128)(2,1)S(1)}, bf16[8,18,1,128]{3,2,1,0:T(2,128)(2,1)S(1)}, u32[]{:S(2)}, u32[]{:S(2)}) collective-permute-start(bf16[8,18,1,128]{3,2,1,0:T(2,128)(2,1)S(1)} %get-tuple-element.17), channel_id=1, source_target_pairs={{1,0},{2,1},{3,2},{4,3},{5,4},{6,5},{7,6},{8,7},{9,8},{10,9},{11,1... | collective-permute-start | bytes 110600 | tf_op jit(solution)/shard_map/ppermute | solution.py:15
Sparse Core Ops, SparseCore 0:
  10.4 60.6 all-gather.2
  73.1 79.7 all-gather.4
where the time goes:
time: 201 us; the launch traced here: 200 us
  waiting for transfers between devices  102 us (51%)
  starting transfers between devices  31.8 us (16%)
  local copies, waits for them, and re-layouts  20.9 us (10%)
  matrix products  14.4 us (7%)
  between operations  13.9 us (7%)
  blocking collectives  9.77 us (5%)
  other arithmetic  7.18 us (4%)
    all_gather x1, waiting for transfers between devices, body(): whole = lax.all_gather(first_act, 'grp', axis=1, tiled=True)  61.1 us
    ppermute x5, starting transfers between devices, with_halo(): before = lax.ppermute(last, axis, up)  21.3 us
    ppermute x5, waiting for transfers between devices, with_halo(): after = lax.ppermute(initial, axis, down)  20.3 us
    all_gather x1, waiting for transfers between devices, middle_conv(): lax.all_gather(mid_filters, 'tile', axis=4, tiled=True)  16.2 us
    unnamed x35, local copies, waits for them, and re-layouts  12.7 us
    ppermute x5, starting transfers between devices, with_halo(): after = lax.ppermute(initial, axis, down)  10.5 us
    all_to_all x1, blocking collectives, body(): lax.all_to_all(filtered, 'grp', split_axis=1, concat_axis=3, tiled=True)  9.77 us
    dot_general x4, matrix products, apply_columns(): jnp.dot(columns[frame_step:frame_step + frames], folded[frame_step], pref...  6.33 us
  transfers between devices with their start and end apart: 12, of which 8 were waited for; matrix products, arithmetic and copies ran while one was open for 10% of the time, Pallas kernels for 0%

commit v1 on v0

--- a/solution.py
+++ b/solution.py
@@ -97,7 +97,10 @@
     widened = with_halo(whole, (("tile", 2),), 1)
     padded = jnp.pad(widened, ((0, 0), (1, 1), (0, 0), (0, 0)))
     filtered = coarse_conv(padded, coarse_filters).astype(jnp.bfloat16)
-    returned = lax.all_to_all(filtered, "grp", split_axis=1, concat_axis=3, tiled=True)
+    returned = jnp.concatenate(
+        lax.all_to_all(jnp.stack(jnp.split(filtered, lax.axis_size("grp"), axis=1)), "grp", 0, 0),
+        axis=3,
+    )
     level_zero = (latent.astype(jnp.float32) + returned.astype(jnp.float32)).astype(jnp.bfloat16)
     reduced = jnp.dot(level_zero, coarse_proj, preferred_element_type=jnp.float32).astype(
         jnp.bfloat16

time: 201 us -> 211 us (1.050)
  waiting for transfers between devices: 102 us -> 109 us
    all_gather x1, waiting for transfers between devices: 16.2 us -> 22.3 us  [middle_conv(): lax.all_gather(mid_filters, 'tile', axis=4, tiled=True)]
    unnamed x35 -> x50, local copies, waits for them, and re-layouts: 12.7 us -> 12.9 us
  transfers between devices with their start and end apart: 12 -> 12, of which waited for: 8 -> 8; matrix products, arithmetic and copies ran while one was open for 10% -> 9% of each run, Pallas kernels for 0% -> 0%
where the time goes in v1:
time: 211 us; the launch traced here: 210 us
  waiting for transfers between devices  109 us (52%)
  starting transfers between devices  32.2 us (15%)
  local copies, waits for them, and re-layouts  22.1 us (10%)
  between operations  15.5 us (7%)
  matrix products  14.4 us (7%)
  blocking collectives  9.77 us (5%)
  other arithmetic  7.22 us (3%)
    all_gather x1, waiting for transfers between devices, body(): whole = lax.all_gather(first_act, 'grp', axis=1, tiled=True)  61.8 us
    all_gather x1, waiting for transfers between devices, middle_conv(): lax.all_gather(mid_filters, 'tile', axis=4, tiled=True)  22.3 us
    ppermute x5, starting transfers between devices, with_halo(): before = lax.ppermute(last, axis, up)  22.3 us
    ppermute x5, waiting for transfers between devices, with_halo(): after = lax.ppermute(initial, axis, down)  20.3 us
    unnamed x50, local copies, waits for them, and re-layouts  12.9 us
    ppermute x5, starting transfers between devices, with_halo(): after = lax.ppermute(initial, axis, down)  9.78 us
    all_to_all x1, blocking collectives, body(): lax.all_to_all(jnp.stack(jnp.split(filtered, lax.axis_size('grp'), axis=1...  9.77 us
    dot_general x4, matrix products, apply_columns(): jnp.dot(columns[frame_step:frame_step + frames], folded[frame_step], pref...  6.33 us
  transfers between devices with their start and end apart: 12, of which 8 were waited for; matrix products, arithmetic and copies ran while one was open for 9% of the time, Pallas kernels for 0%

profile of v1, /device:TPU:7, one launch (start us, length us, event | category | flops | bytes accessed | tf_op | source)
XLA Modules:
  0.0 210.0 jit_solution(6165011166375959016)
XLA Ops:
  8.4 1.6 fusion.33
  10.1 61.8 %all-gather.3.cloned.1.call-done = bf16[8,64,2,512]{3,0,2,1:T(8,128)(2,1)} async-done(((bf16[8,4,2,512]{3,0,2,1:T(8,128)(2,1)}), bf16[8,64,2,512]{3,0,2,1:T(8,128)(2,1)}) %all-gather.3.cloned.1.call-update) | async-done | bytes 1048592 | tf_op jit(solution)/shard_map/all_gather | solution.py:96
  71.9 1.8 copy.37
  74.8 5.0 %collective-permute-start = (bf16[8,64,1,512]{3,1,2,0:T(8,128)(2,1)}, bf16[8,64,1,512]{3,1,2,0:T(8,128)(2,1)S(1)}, u32[]{:S(2)}, u32[]{:S(2)}) collective-permute-start(bf16[8,64,1,512]{3,1,2,0:T(8,128)(2,1)} %get-tuple-element.8), channel_id=1, source_target_pairs={{0,1},{1,2},{2,3},{3,4},{4,5},{5,6},{6,7},{7,8},{8,9},{9,10},{10,1... | collective-permute-start | bytes 1572872 | tf_op jit(solution)/shard_map/ppermute | solution.py:14
  79.8 1.9 collective-permute-start.1
  81.9 4.4 %collective-permute-done = bf16[8,64,1,512]{3,1,2,0:T(8,128)(2,1)S(1)} collective-permute-done((bf16[8,64,1,512]{3,1,2,0:T(8,128)(2,1)}, bf16[8,64,1,512]{3,1,2,0:T(8,128)(2,1)S(1)}, u32[]{:S(2)}, u32[]{:S(2)}) %collective-permute-start) | collective-permute-done | bytes 524320 | tf_op jit(solution)/shard_map/ppermute | solution.py:14
  86.3 4.3 %collective-permute-done.1 = bf16[8,64,1,512]{3,1,2,0:T(8,128)(2,1)S(1)} collective-permute-done((bf16[8,64,1,512]{3,1,2,0:T(8,128)(2,1)}, bf16[8,64,1,512]{3,1,2,0:T(8,128)(2,1)S(1)}, u32[]{:S(2)}, u32[]{:S(2)}) %collective-permute-start.1) | collective-permute-done | bytes 524320 | tf_op jit(solution)/shard_map/ppermute | solution.py:15
  91.6 1.4 fusion.47
  93.0 1.4 fusion.50
  94.5 1.4 fusion.51
  95.9 2.5 %fusion.24 = bf16[8,64,2,32]{3,1,2,0:T(8,128)(2,1)S(1)} fusion(f32[8,66,4,288]{3,1,2,0:T(8,128)S(1)} %fusion.47, f32[8,66,4,288]{3,1,2,0:T(8,128)S(1)} %fusion.51, f32[8,66,4,288]{3,1,2,0:T(8,128)S(1)} %fusion.50), kind=kLoop, calls=%fused_computation.35 | loop fusion | flops 884736 | bytes 3604480 | tf_op jit(solution)/shard_map/convert_element_type | solution.py:99
  99.1 9.8 %all_to_all.5 = bf16[16,2,1024]{2,1,0:T(2,128)(2,1)S(1)} all-to-all(bf16[16,2,1024]{2,1,0:T(2,128)(2,1)S(1)} %reshape.90), channel_id=1, replica_groups=mesh['grp'=16,'tile'=32] {'grp'}, dimensions={0} | all-to-all | bytes 131072 | tf_op jit(solution)/shard_map/all_to_all | solution.py:101
  110.4 3.7 %collective-permute-start.2 = (bf16[8,1,4,256]{3,2,1,0:T(4,128)(2,1)S(1)}, bf16[8,1,4,256]{3,2,1,0:T(4,128)(2,1)S(1)}, u32[]{:S(2)}, u32[]{:S(2)}) collective-permute-start(bf16[8,1,4,256]{3,2,1,0:T(4,128)(2,1)S(1)} %get-tuple-element.23), channel_id=1, source_target_pairs={{0,32},{32,64},{64,96},{96,128},{128,160},{160,192},{192,224},{224... | collective-permute-start | bytes 49160 | tf_op jit(solution)/shard_map/ppermute | solution.py:14
  114.0 1.9 collective-permute-start.3
  116.1 4.6 %collective-permute-done.3 = bf16[8,1,4,256]{3,2,1,0:T(4,128)(2,1)S(1)} collective-permute-done((bf16[8,1,4,256]{3,2,1,0:T(4,128)(2,1)S(1)}, bf16[8,1,4,256]{3,2,1,0:T(4,128)(2,1)S(1)}, u32[]{:S(2)}, u32[]{:S(2)}) %collective-permute-start.3) | collective-permute-done | bytes 16416 | tf_op jit(solution)/shard_map/ppermute | solution.py:15
  120.8 4.7 %collective-permute-start.4 = (bf16[8,10,1,256]{3,2,1,0:T(2,128)(2,1)S(1)}, bf16[8,10,1,256]{3,2,1,0:T(2,128)(2,1)S(1)}, u32[]{:S(2)}, u32[]{:S(2)}) collective-permute-start(bf16[8,10,1,256]{3,2,1,0:T(2,128)(2,1)S(1)} %get-tuple-element.20), channel_id=1, source_target_pairs={{0,1},{1,2},{2,3},{3,4},{4,5},{5,6},{6,7},{7,8},{8,9},{9,10},{10,1... | collective-permute-start | bytes 122888 | tf_op jit(solution)/shard_map/ppermute | solution.py:14
  125.5 2.1 %collective-permute-start.5 = (bf16[8,10,1,256]{3,2,1,0:T(2,128)(2,1)S(1)}, bf16[8,10,1,256]{3,2,1,0:T(2,128)(2,1)S(1)}, u32[]{:S(2)}, u32[]{:S(2)}) collective-permute-start(bf16[8,10,1,256]{3,2,1,0:T(2,128)(2,1)S(1)} %get-tuple-element.21), channel_id=1, source_target_pairs={{1,0},{2,1},{3,2},{4,3},{5,4},{6,5},{7,6},{8,7},{9,8},{10,9},{11,1... | collective-permute-start | bytes 122888 | tf_op jit(solution)/shard_map/ppermute | solution.py:15
  128.0 3.2 %collective-permute-done.5 = bf16[8,10,1,256]{3,2,1,0:T(2,128)(2,1)S(1)} collective-permute-done((bf16[8,10,1,256]{3,2,1,0:T(2,128)(2,1)S(1)}, bf16[8,10,1,256]{3,2,1,0:T(2,128)(2,1)S(1)}, u32[]{:S(2)}, u32[]{:S(2)}) %collective-permute-start.5) | collective-permute-done | bytes 40992 | tf_op jit(solution)/shard_map/ppermute | solution.py:15
  138.7 22.3 %all-gather.5.cloned.1.call-done = bf16[3,3,3,256,256]{3,4,2,1,0:T(8,128)(2,1)} async-done(((bf16[3,3,3,256,8]{3,4,2,1,0:T(8,128)(2,1)}), bf16[3,3,3,256,256]{3,4,2,1,0:T(8,128)(2,1)}) %all-gather.5.cloned.1.call-update) | async-done | bytes 3538960 | tf_op jit(solution)/shard_map/all_gather | solution.py:91
  161.0 3.3 %fusion.40 = (bf16[1,3,3,256,256]{3,4,2,1,0:T(8,128)(2,1)S(1)}, bf16[1,3,3,256,256]{3,4,2,1,0:T(8,128)(2,1)S(1)}, bf16[1,3,3,256,256]{3,4,2,1,0:T(8,128)(2,1)}) fusion(bf16[3,3,3,256,256]{3,4,2,1,0:T(8,128)(2,1)} %all-gather.5.cloned.1.call-done), kind=kLoop, calls=%fused_computation.142 | loop fusion | bytes 7077888 | tf_op jit(solution)/shard_map/slice | solution.py:55
  164.3 2.4 %copy.60 = bf16[1,3,3,256,256]{4,3,2,1,0:T(8,128)(2,1)} copy(bf16[1,3,3,256,256]{3,4,2,1,0:T(8,128)(2,1)} %get-tuple-element.7) | data formatting | bytes 2359296
  166.7 1.6 copy.61
  169.0 2.4 %fusion.48 = f32[8,8,4,256]{3,2,1,0:T(4,128)S(1)} fusion(bf16[10,8,4,2304]{3,2,1,0:T(4,128)(2,1)} %slice_dynamic-update-slice_fusion.9, bf16[2304,256,1,1]{1,0,3,2:T(8,128)(2,1)} %bitcast.174), kind=kOutput, calls=%fused_computation.150 | convolution fusion | flops 301989888 | bytes 2916352 | tf_op jit(solution)/shard_map/dot_general | solution.py:51
  171.4 2.0 convolution_add_fusion.3
  173.4 2.1 fusion.14
  176.3 4.1 %collective-permute-start.6 = (bf16[8,1,8,128]{3,2,1,0:T(8,128)(2,1)S(1)}, bf16[8,1,8,128]{3,2,1,0:T(8,128)(2,1)S(1)}, u32[]{:S(2)}, u32[]{:S(2)}) collective-permute-start(bf16[8,1,8,128]{3,2,1,0:T(8,128)(2,1)S(1)} %get-tuple-element.18), channel_id=1, source_target_pairs={{0,32},{32,64},{64,96},{96,128},{128,160},{160,192},{192,224},{224... | collective-permute-start | bytes 49160 | tf_op jit(solution)/shard_map/ppermute | solution.py:14
  180.4 1.9 collective-permute-start.7
  182.3 4.7 %collective-permute-done.7 = bf16[8,1,8,128]{3,2,1,0:T(8,128)(2,1)S(1)} collective-permute-done((bf16[8,1,8,128]{3,2,1,0:T(8,128)(2,1)S(1)}, bf16[8,1,8,128]{3,2,1,0:T(8,128)(2,1)S(1)}, u32[]{:S(2)}, u32[]{:S(2)}) %collective-permute-start.7) | collective-permute-done | bytes 16416 | tf_op jit(solution)/shard_map/ppermute | solution.py:15
  187.1 4.8 %collective-permute-start.8 = (bf16[8,18,1,128]{3,2,1,0:T(2,128)(2,1)S(1)}, bf16[8,18,1,128]{3,2,1,0:T(2,128)(2,1)S(1)}, u32[]{:S(2)}, u32[]{:S(2)}) collective-permute-start(bf16[8,18,1,128]{3,2,1,0:T(2,128)(2,1)S(1)} %get-tuple-element.16), channel_id=1, source_target_pairs={{0,1},{1,2},{2,3},{3,4},{4,5},{5,6},{6,7},{7,8},{8,9},{9,10},{10,1... | collective-permute-start | bytes 110600 | tf_op jit(solution)/shard_map/ppermute | solution.py:14
  191.9 1.9 collective-permute-start.9
  194.0 3.6 %collective-permute-done.9 = bf16[8,18,1,128]{3,2,1,0:T(2,128)(2,1)S(1)} collective-permute-done((bf16[8,18,1,128]{3,2,1,0:T(2,128)(2,1)S(1)}, bf16[8,18,1,128]{3,2,1,0:T(2,128)(2,1)S(1)}, u32[]{:S(2)}, u32[]{:S(2)}) %collective-permute-start.9) | collective-permute-done | bytes 36896 | tf_op jit(solution)/shard_map/ppermute | solution.py:15
  201.0 1.5 fusion.12
  (97 shorter events, 18.3 us)
Async XLA Ops:
  7.4 102.3 %copy-start = (bf16[512,256]{1,0:T(8,128)(2,1)S(1)}, bf16[512,256]{1,0:T(8,128)(2,1)}, u32[]{:S(2)}) copy-start(bf16[512,256]{1,0:T(8,128)(2,1)} %param.10) | copy-start | bytes 786436
  7.4 74.4 %copy-start.2 = (bf16[3,3,3,512,32]{3,4,2,1,0:T(8,128)(2,1)S(1)}, bf16[3,3,3,512,32]{3,4,2,1,0:T(8,128)(2,1)}, u32[]{:S(2)}) copy-start(bf16[3,3,3,512,32]{3,4,2,1,0:T(8,128)(2,1)} %param.7) | copy-start | bytes 2654212
  7.4 64.5 %all-gather.3.cloned.1.call-start = ((), (), s32[]{:S(2)}) async-start(), calls=%async_computation.1 | async-start | bytes 1114112 | tf_op jit(solution)/shard_map/all_gather | solution.py:96
  10.0 151.0 %all-gather.5.cloned.1.call-start = ((), (), s32[]{:S(2)}) async-start(), calls=%async_computation.2 | async-start | bytes 3649536 | tf_op jit(solution)/shard_map/all_gather | solution.py:91
  74.8 11.5 %collective-permute-start = (bf16[8,64,1,512]{3,1,2,0:T(8,128)(2,1)}, bf16[8,64,1,512]{3,1,2,0:T(8,128)(2,1)S(1)}, u32[]{:S(2)}, u32[]{:S(2)}) collective-permute-start(bf16[8,64,1,512]{3,1,2,0:T(8,128)(2,1)} %get-tuple-element.8), channel_id=1, source_target_pairs={{0,1},{1,2},{2,3},{3,4},{4,5},{5,6},{6,7},{7,8},{8,9},{9,10},{10,1... | collective-permute-start | bytes 1572872 | tf_op jit(solution)/shard_map/ppermute | solution.py:14
  79.8 10.7 %collective-permute-start.1 = (bf16[8,64,1,512]{3,1,2,0:T(8,128)(2,1)}, bf16[8,64,1,512]{3,1,2,0:T(8,128)(2,1)S(1)}, u32[]{:S(2)}, u32[]{:S(2)}) collective-permute-start(bf16[8,64,1,512]{3,1,2,0:T(8,128)(2,1)} %get-tuple-element.9), channel_id=1, source_target_pairs={{1,0},{2,1},{3,2},{4,3},{5,4},{6,5},{7,6},{8,7},{9,8},{10,9},{11,1... | collective-permute-start | bytes 1572872 | tf_op jit(solution)/shard_map/ppermute | solution.py:15
  98.4 11.3 %copy-start.4 = (bf16[8,4,2,512]{3,2,1,0:T(2,128)(2,1)S(1)}, bf16[8,4,2,512]{3,2,1,0:T(2,128)(2,1)}, u32[]{:S(2)}) copy-start(bf16[8,4,2,512]{3,2,1,0:T(2,128)(2,1)} %param.6) | copy-start | bytes 196612
  110.4 5.6 %collective-permute-start.2 = (bf16[8,1,4,256]{3,2,1,0:T(4,128)(2,1)S(1)}, bf16[8,1,4,256]{3,2,1,0:T(4,128)(2,1)S(1)}, u32[]{:S(2)}, u32[]{:S(2)}) collective-permute-start(bf16[8,1,4,256]{3,2,1,0:T(4,128)(2,1)S(1)} %get-tuple-element.23), channel_id=1, source_target_pairs={{0,32},{32,64},{64,96},{96,128},{128,160},{160,192},{192,224},{224... | collective-permute-start | bytes 49160 | tf_op jit(solution)/shard_map/ppermute | solution.py:14
  114.0 6.6 %collective-permute-start.3 = (bf16[8,1,4,256]{3,2,1,0:T(4,128)(2,1)S(1)}, bf16[8,1,4,256]{3,2,1,0:T(4,128)(2,1)S(1)}, u32[]{:S(2)}, u32[]{:S(2)}) collective-permute-start(bf16[8,1,4,256]{3,2,1,0:T(4,128)(2,1)S(1)} %get-tuple-element.22), channel_id=1, source_target_pairs={{32,0},{64,32},{96,64},{128,96},{160,128},{192,160},{224,192},{256... | collective-permute-start | bytes 49160 | tf_op jit(solution)/shard_map/ppermute | solution.py:15
  120.8 7.3 %collective-permute-start.4 = (bf16[8,10,1,256]{3,2,1,0:T(2,128)(2,1)S(1)}, bf16[8,10,1,256]{3,2,1,0:T(2,128)(2,1)S(1)}, u32[]{:S(2)}, u32[]{:S(2)}) collective-permute-start(bf16[8,10,1,256]{3,2,1,0:T(2,128)(2,1)S(1)} %get-tuple-element.20), channel_id=1, source_target_pairs={{0,1},{1,2},{2,3},{3,4},{4,5},{5,6},{6,7},{7,8},{8,9},{9,10},{10,1... | collective-permute-start | bytes 122888 | tf_op jit(solution)/shard_map/ppermute | solution.py:14
  125.5 5.8 %collective-permute-start.5 = (bf16[8,10,1,256]{3,2,1,0:T(2,128)(2,1)S(1)}, bf16[8,10,1,256]{3,2,1,0:T(2,128)(2,1)S(1)}, u32[]{:S(2)}, u32[]{:S(2)}) collective-permute-start(bf16[8,10,1,256]{3,2,1,0:T(2,128)(2,1)S(1)} %get-tuple-element.21), channel_id=1, source_target_pairs={{1,0},{2,1},{3,2},{4,3},{5,4},{6,5},{7,6},{8,7},{9,8},{10,9},{11,1... | collective-permute-start | bytes 122888 | tf_op jit(solution)/shard_map/ppermute | solution.py:15
  169.0 2.4 %copy-start.1 = (bf16[1,3,3,256,256]{4,3,2,1,0:T(8,128)(2,1)S(1)}, bf16[1,3,3,256,256]{4,3,2,1,0:T(8,128)(2,1)}, u32[]{:S(2)}) copy-start(bf16[1,3,3,256,256]{4,3,2,1,0:T(8,128)(2,1)} %copy.61) | copy-start | bytes 3538948
  173.4 2.1 %copy-start.5 = (bf16[256,128]{1,0:T(8,128)(2,1)S(1)}, bf16[256,128]{1,0:T(8,128)(2,1)}, u32[]{:S(2)}) copy-start(bf16[256,128]{1,0:T(8,128)(2,1)} %param.11) | copy-start | bytes 196612
  173.4 20.4 %copy-start.3 = (bf16[3,3,3,128,128]{4,3,2,1,0:T(8,128)(2,1)S(1)}, bf16[3,3,3,128,128]{4,3,2,1,0:T(8,128)(2,1)}, u32[]{:S(2)}) copy-start(bf16[3,3,3,128,128]{4,3,2,1,0:T(8,128)(2,1)} %param.9) | copy-start | bytes 2654212
  176.3 6.1 %collective-permute-start.6 = (bf16[8,1,8,128]{3,2,1,0:T(8,128)(2,1)S(1)}, bf16[8,1,8,128]{3,2,1,0:T(8,128)(2,1)S(1)}, u32[]{:S(2)}, u32[]{:S(2)}) collective-permute-start(bf16[8,1,8,128]{3,2,1,0:T(8,128)(2,1)S(1)} %get-tuple-element.18), channel_id=1, source_target_pairs={{0,32},{32,64},{64,96},{96,128},{128,160},{160,192},{192,224},{224... | collective-permute-start | bytes 49160 | tf_op jit(solution)/shard_map/ppermute | solution.py:14
  180.4 6.6 %collective-permute-start.7 = (bf16[8,1,8,128]{3,2,1,0:T(8,128)(2,1)S(1)}, bf16[8,1,8,128]{3,2,1,0:T(8,128)(2,1)S(1)}, u32[]{:S(2)}, u32[]{:S(2)}) collective-permute-start(bf16[8,1,8,128]{3,2,1,0:T(8,128)(2,1)S(1)} %get-tuple-element.19), channel_id=1, source_target_pairs={{32,0},{64,32},{96,64},{128,96},{160,128},{192,160},{224,192},{256... | collective-permute-start | bytes 49160 | tf_op jit(solution)/shard_map/ppermute | solution.py:15
  187.1 6.9 %collective-permute-start.8 = (bf16[8,18,1,128]{3,2,1,0:T(2,128)(2,1)S(1)}, bf16[8,18,1,128]{3,2,1,0:T(2,128)(2,1)S(1)}, u32[]{:S(2)}, u32[]{:S(2)}) collective-permute-start(bf16[8,18,1,128]{3,2,1,0:T(2,128)(2,1)S(1)} %get-tuple-element.16), channel_id=1, source_target_pairs={{0,1},{1,2},{2,3},{3,4},{4,5},{5,6},{6,7},{7,8},{8,9},{9,10},{10,1... | collective-permute-start | bytes 110600 | tf_op jit(solution)/shard_map/ppermute | solution.py:14
  191.9 5.7 %collective-permute-start.9 = (bf16[8,18,1,128]{3,2,1,0:T(2,128)(2,1)S(1)}, bf16[8,18,1,128]{3,2,1,0:T(2,128)(2,1)S(1)}, u32[]{:S(2)}, u32[]{:S(2)}) collective-permute-start(bf16[8,18,1,128]{3,2,1,0:T(2,128)(2,1)S(1)} %get-tuple-element.17), channel_id=1, source_target_pairs={{1,0},{2,1},{3,2},{4,3},{5,4},{6,5},{7,6},{8,7},{9,8},{10,9},{11,1... | collective-permute-start | bytes 110600 | tf_op jit(solution)/shard_map/ppermute | solution.py:15
Sparse Core Ops, SparseCore 0:
  11.2 60.6 all-gather.2
Sparse Core Ops, SparseCore 1:
  81.9 79.1 all-gather.4
